TPU v7x, 32 devices: a whole 2x2x4 slice. The times are simulated.
32 devices in a mesh: clip: 2 (over x), tile: 16 (over z, y, core).
Axes of the slice: x: 2, y: 2, z: 4, core: 2. Of those that a mesh axis runs over, the one named last changes fastest.
Arguments:
- frames: bfloat16 [8, 32, 128, 1024], P('clip', 'tile'), parts along dimension 0, may hold values from -40 to 40
- keyframes: bfloat16 [4, 32, 128, 1024], P('clip', 'tile'), parts along dimension 0, may hold values from -40 to 40
- matches: int32 [16, 8, 4], P('tile', 'clip'), parts along dimension 1, may hold values from 0 to 5, as said below
- counts: int32 [16, 8], P('tile', 'clip'), parts along dimension 1, may hold values from 1 to 4, as said below
- w_query: bfloat16 [1024, 1024], replicated, may hold values from -1 to 1
- w_key: bfloat16 [1024, 1024], replicated, may hold values from -1 to 1
- w_value: bfloat16 [1024, 1024], replicated, may hold values from -0.1875 to 0.1875
- w_out: bfloat16 [1024, 1024], replicated, may hold values from -0.1875 to 0.1875
Outputs:
- mixed: bfloat16 [8, 32, 128, 1024], P('clip', None, 'tile'), parts along dimension 0
There are 2 independent parts, one for each index of `clip`. A program takes and returns all parts, laid end to end along the dimension named above; an argument that names none is the same for every part. Nothing has to cross between parts.
Inputs may be any that keep to these rules, and one draw needn't show every extreme that they name: `matches`: every entry names a candidate whose block lies inside the image; the entries of one list are distinct, and entry 0 is candidate 1 (keyframe 0's block at the reader's own tile). Entries past the count are valid but unused. `counts`: in every frame some tile uses 4 entries.
All inputs are finite; a program needn't handle non-finite values.
Results may differ from a plain program's by a relative error of at most 0.0095.
Values may be sent and summed in bfloat16 or wider, within the bound.
A program may use at most 128 MiB of HBM per device.

v0:
```python
import jax
import jax.numpy as jnp
from jax import lax
from jax.sharding import PartitionSpec as P

HEADS = 16


def with_halo(cells, sides, width):
    for axis, dim in sides:
        count = lax.axis_size(axis)
        ends = count - 1
        head = lax.slice_in_dim(cells, 0, width, axis=dim)
        tail = lax.slice_in_dim(cells, cells.shape[dim] - width, cells.shape[dim], axis=dim)
        cells = jnp.concatenate(
            [
                lax.ppermute(tail, axis, [(i, (i + 1) % count) for i in range(ends)]),
                cells,
                lax.ppermute(head, axis, [((i + 1) % count, i) for i in range(ends)]),
            ],
            axis=dim,
        )
    return cells


def attend(queries, keys, values, allowed):
    head_dim = queries.shape[2]
    scores = jnp.einsum(
        "qhd,khd->hqk", queries, keys, preferred_element_type=jnp.float32
    ) * head_dim ** (-0.5)
    scores = jnp.where(allowed[None, None, :], scores, -jnp.inf)
    row_max = jnp.max(scores, axis=-1, keepdims=True)
    exp_terms = jnp.exp(scores - row_max)
    probabilities = (exp_terms / jnp.sum(exp_terms, axis=-1, keepdims=True)).astype(jnp.bfloat16)
    context = jnp.einsum("hqk,khd->qhd", probabilities, values, preferred_element_type=jnp.float32)
    return context.astype(jnp.bfloat16)


def shards(frames, keyframes, matches, counts, w_query, w_key, w_value, w_out):
    frame_count, row_count, col_count, model_dim = frames.shape
    key_count = keyframes.shape[0]
    block_len = row_count * col_count
    head_count = HEADS
    head_dim = model_dim // head_count
    w_pair = jnp.concatenate([w_key, w_value], axis=1)
    own_pairs = jnp.dot(
        keyframes.reshape(key_count * block_len, model_dim),
        w_pair,
        preferred_element_type=jnp.float32,
    ).astype(jnp.bfloat16)
    nearby = with_halo(own_pairs.reshape(1, key_count, block_len, 2 * model_dim), (("tile", 0),), 1)
    nearby = nearby.reshape(3 * key_count, block_len, 2, head_count, head_dim)
    key_table = nearby[:, :, 0]
    value_table = nearby[:, :, 1]
    query = jnp.dot(
        frames.reshape(frame_count * block_len, model_dim),
        w_query,
        preferred_element_type=jnp.float32,
    ).astype(jnp.bfloat16)
    query = query.reshape(frame_count, block_len, head_count, head_dim)
    candidates = matches[0]
    live_counts = counts[0]
    slot_count = candidates.shape[1]
    flat_index = candidates % 3 * key_count + candidates // 3
    slot_ids = jnp.arange(slot_count, dtype=jnp.int32)

    def per_frame(inputs):
        queries, chosen, live_now = inputs
        used = slot_ids < live_now
        keys = key_table[chosen].reshape(slot_count * block_len, head_count, head_dim)
        values = value_table[chosen].reshape(slot_count * block_len, head_count, head_dim)
        allowed = jnp.repeat(used, block_len)
        return attend(queries, keys, values, allowed)

    context = lax.map(per_frame, (query, flat_index, live_counts))
    context = context.reshape(frame_count * block_len, model_dim)
    update = jnp.dot(context, w_out, preferred_element_type=jnp.float32)
    mixed = frames.reshape(frame_count * block_len, model_dim).astype(jnp.float32) + update
    mixed = mixed.astype(jnp.bfloat16).reshape(frame_count, row_count, col_count, model_dim)
    return lax.all_to_all(mixed, "tile", split_axis=2, concat_axis=1, tiled=True)


def solution(mesh):
    placed = (
        P("clip", "tile", None, None),
        P("clip", "tile", None, None),
        P("tile", "clip", None),
        P("tile", "clip"),
        P(),
        P(),
        P(),
        P(),
    )
    return jax.shard_map(
        shards, mesh=mesh, in_specs=placed, out_specs=P("clip", None, "tile", None), check_vma=False
    )
```

profile of v0, /device:TPU:0, one launch (start us, length us, event | category | flops | bytes accessed | tf_op | source)
XLA Modules:
  0.0 364.8 jit_solution(17891498973158065592)
XLA Ops:
  0.0 6.3 %fusion.31 = bf16[2048,512]{0,1:T(8,128)(2,1)} fusion(bf16[512,1024]{1,0:T(8,128)(2,1)} %bitcast.88, bf16[1024,1024]{1,0:T(8,128)(2,1)} %param.16, bf16[1024,1024]{1,0:T(8,128)(2,1)} %param.15), kind=kOutput, calls=%fused_computation.37 | convolution fusion | flops 2156920832 | bytes 7340032 | tf_op jit(solution)/shard_map/dot_general | solution.py:46
  6.3 3.9 %copy.26 = bf16[1,2,256,2048]{2,3,1,0:T(8,128)(2,1)} copy(bf16[1,2,256,2048]{3,2,1,0:T(8,128)(2,1)} %bitcast.85) | data formatting | bytes 4194304 | tf_op jit(solution)/shard_map/reshape | solution.py:51
  10.3 3.7 %collective-permute-start = (bf16[1,2,256,2048]{2,3,1,0:T(8,128)(2,1)}, bf16[1,2,256,2048]{2,3,1,0:T(8,128)(2,1)}, u32[]{:S(2)}, u32[]{:S(2)}) collective-permute-start(bf16[1,2,256,2048]{2,3,1,0:T(8,128)(2,1)} %copy.26), channel_id=1, source_target_pairs={{0,1},{1,2},{2,3},{3,4},{4,5},{5,6},{6,7},{7,8},{8,9},{9,10},{10,1... | collective-permute-start | bytes 6291464 | tf_op jit(solution)/shard_map/ppermute | solution.py:17
  14.0 1.3 collective-permute-start.1
  15.3 5.2 %convolution_convert_fusion = bf16[1024,1024]{1,0:T(8,128)(2,1)} fusion(bf16[1024,1024]{1,0:T(8,128)(2,1)} %bitcast.86, bf16[1024,1024]{1,0:T(8,128)(2,1)S(1)} %copy-done), kind=kOutput, calls=%fused_computation.38 | convolution fusion | flops 2148532224 | bytes 6291456 | tf_op jit(solution)/shard_map/dot_general | solution.py:55
  20.5 6.4 %reshape.97 = bf16[4,256,16,64]{3,2,1,0:T(8,128)(2,1)} reshape(bf16[1024,1024]{1,0:T(8,128)(2,1)} %convolution_convert_fusion) | data formatting | bytes 4194304 | tf_op jit(solution)/shard_map/reshape | solution.py:60
  26.9 4.9 %copy.31 = bf16[4,256,16,64]{1,3,2,0:T(8,128)(2,1)S(1)} copy(bf16[4,256,16,64]{3,2,1,0:T(8,128)(2,1)} %reshape.97) | data formatting | bytes 4194304
  31.8 3.7 %pad_maximum_fusion = bf16[3,2,256,2048]{2,3,1,0:T(8,128)(2,1)S(1)} fusion(bf16[1,2,256,2048]{2,3,1,0:T(8,128)(2,1)} %collective-permute-done.1, bf16[1,2,256,2048]{2,3,1,0:T(8,128)(2,1)} %copy.26, bf16[1,2,256,2048]{2,3,1,0:T(8,128)(2,1)} %collective-permute-done), kind=kLoop, calls=%fused_computation.29 | loop fusion | flops 6291456 | bytes 12582912 | tf_op jit(solution)/shard_map/concatenate | solution.py:15
  35.5 3.2 slice_bitcast_fusion
  38.7 8.5 %copy.30 = bf16[6,256,16,64]{3,2,1,0:T(8,128)(2,1)} copy(bf16[6,256,16,64]{1,3,2,0:T(8,128)(2,1)} %get-tuple-element.102) | data formatting | bytes 6291456
  47.2 8.5 %copy.32 = bf16[6,256,16,64]{3,2,1,0:T(8,128)(2,1)} copy(bf16[6,256,16,64]{1,3,2,0:T(8,128)(2,1)} %get-tuple-element.101) | data formatting | bytes 6291456
  55.7 214.4 %while.11 = (s32[]{:T(128)}, bf16[4,256,16,64]{1,3,2,0:T(8,128)(2,1)}, s32[4,4]{1,0:T(4,128)S(1)}, bf16[6,256,16,64]{3,2,1,0:T(8,128)(2,1)}, s32[4]{0:T(128)S(1)...) while((s32[]{:T(128)}, ...), condition=%wide.region_3.4_spmd.clone, body=%wide.region_0.3_spmd.clone.sunk | while | flops 1107560448 | bytes 82879176 | solution.py:75
  55.7 5.8 %gather_fusion = bf16[4,256,16,64]{3,2,1,0:T(8,128)(2,1)} fusion(bf16[6,256,16,64]{3,2,1,0:T(8,128)(2,1)} %get-tuple-element.172, s32[1024]{0:T(1024)S(1)} %pad_clamp_fusion.2), kind=kCustom, calls=%fused_computation.1.clone.clone.1 | custom fusion | bytes 4194320 | tf_op jit(solution)/shard_map/while/body/eval_jaxpr/gather | solution.py:70
  61.5 10.8 %fusion.57 = f32[16,256,1024]{2,1,0:T(8,128)} fusion(bf16[1024,16,64]{2,1,0:T(8,128)(2,1)} %bitcast.78, bf16[4,256,16,64]{1,3,2,0:T(8,128)(2,1)S(1)} %get-tuple-element.171, s32[]{:T(128)} %get-tuple-element.158), kind=kOutput, calls=%fused_computation.13.clone.1 | convolution fusion | flops 536870912 | bytes 19398660 | tf_op jit(solution)/shard_map/while/body/eval_jaxpr/qhd,khd->hqk/dot_general | solution.py:28
  72.3 0.7 dynamic_slice.31
  73.0 0.7 iota_compare_fusion.2
  73.7 0.1 broadcast_in_dim.54
  73.7 18.3 %fusion.58 = (f32[16,256]{1,0:T(8,128)S(1)}, f32[16,256,1024]{2,1,0:T(8,128)}) fusion(f32[16,256,1024]{2,1,0:T(8,128)} %fusion.57, pred[1024]{0:T(1024)(128)(4,1)S(1)} %broadcast_in_dim.55), kind=kOutput, calls=%fused_computation.50.clone.1 | output fusion | flops 25166848 | bytes 33571840 | tf_op jit(solution)/shard_map/while/body/eval_jaxpr/sub | solution.py:33
  92.1 5.8 %gather_fusion.1 = bf16[4,256,16,64]{3,2,1,0:T(8,128)(2,1)} fusion(bf16[6,256,16,64]{3,2,1,0:T(8,128)(2,1)} %get-tuple-element.169, s32[1024]{0:T(1024)S(1)} %pad_clamp_fusion.2), kind=kCustom, calls=%fused_computation.clone.clone.1 | custom fusion | bytes 4194320 | tf_op jit(solution)/shard_map/while/body/eval_jaxpr/gather | solution.py:71
  97.9 11.5 %fusion.59 = bf16[4,256,16,64]{1,3,2,0:T(8,128)(2,1)} fusion(bf16[4,256,16,64]{1,3,2,0:T(8,128)(2,1)} %get-tuple-element.159, s32[]{:T(128)} %get-tuple-element.158, f32[16,256,1024]{2,1,0:T(8,128)} %get-tuple-element.148, f32[16,256]{1,0:T(8,128)S(1)} %get-tuple-element.149, bf16[1024,16,64]{2,1,0:T(8,128)(2,1)} %bitcast.79), kind=kOutput, calls=%fused_computation.17.clone.1 | convolution fusion | flops 545521664 | bytes 21512704 | tf_op jit(solution)/shard_map/while/body/eval_jaxpr/hqk,khd->qhd/dot_general | solution.py:35
  109.3 5.8 %gather_fusion = bf16[4,256,16,64]{3,2,1,0:T(8,128)(2,1)} fusion(bf16[6,256,16,64]{3,2,1,0:T(8,128)(2,1)} %get-tuple-element.172, s32[1024]{0:T(1024)S(1)} %pad_clamp_fusion.2), kind=kCustom, calls=%fused_computation.1.clone.clone.1 | custom fusion | bytes 4194320 | tf_op jit(solution)/shard_map/while/body/eval_jaxpr/gather | solution.py:70
  115.1 10.8 %fusion.57 = f32[16,256,1024]{2,1,0:T(8,128)} fusion(bf16[1024,16,64]{2,1,0:T(8,128)(2,1)} %bitcast.78, bf16[4,256,16,64]{1,3,2,0:T(8,128)(2,1)S(1)} %get-tuple-element.171, s32[]{:T(128)} %get-tuple-element.158), kind=kOutput, calls=%fused_computation.13.clone.1 | convolution fusion | flops 536870912 | bytes 19398660 | tf_op jit(solution)/shard_map/while/body/eval_jaxpr/qhd,khd->hqk/dot_general | solution.py:28
  125.9 0.7 dynamic_slice.31
  126.6 0.7 iota_compare_fusion.2
  127.2 0.1 broadcast_in_dim.54
  127.3 18.3 %fusion.58 = (f32[16,256]{1,0:T(8,128)S(1)}, f32[16,256,1024]{2,1,0:T(8,128)}) fusion(f32[16,256,1024]{2,1,0:T(8,128)} %fusion.57, pred[1024]{0:T(1024)(128)(4,1)S(1)} %broadcast_in_dim.55), kind=kOutput, calls=%fused_computation.50.clone.1 | output fusion | flops 25166848 | bytes 33571840 | tf_op jit(solution)/shard_map/while/body/eval_jaxpr/sub | solution.py:33
  145.7 5.8 %gather_fusion.1 = bf16[4,256,16,64]{3,2,1,0:T(8,128)(2,1)} fusion(bf16[6,256,16,64]{3,2,1,0:T(8,128)(2,1)} %get-tuple-element.169, s32[1024]{0:T(1024)S(1)} %pad_clamp_fusion.2), kind=kCustom, calls=%fused_computation.clone.clone.1 | custom fusion | bytes 4194320 | tf_op jit(solution)/shard_map/while/body/eval_jaxpr/gather | solution.py:71
  151.5 11.5 %fusion.59 = bf16[4,256,16,64]{1,3,2,0:T(8,128)(2,1)} fusion(bf16[4,256,16,64]{1,3,2,0:T(8,128)(2,1)} %get-tuple-element.159, s32[]{:T(128)} %get-tuple-element.158, f32[16,256,1024]{2,1,0:T(8,128)} %get-tuple-element.148, f32[16,256]{1,0:T(8,128)S(1)} %get-tuple-element.149, bf16[1024,16,64]{2,1,0:T(8,128)(2,1)} %bitcast.79), kind=kOutput, calls=%fused_computation.17.clone.1 | convolution fusion | flops 545521664 | bytes 21512704 | tf_op jit(solution)/shard_map/while/body/eval_jaxpr/hqk,khd->qhd/dot_general | solution.py:35
  162.9 5.8 %gather_fusion = bf16[4,256,16,64]{3,2,1,0:T(8,128)(2,1)} fusion(bf16[6,256,16,64]{3,2,1,0:T(8,128)(2,1)} %get-tuple-element.172, s32[1024]{0:T(1024)S(1)} %pad_clamp_fusion.2), kind=kCustom, calls=%fused_computation.1.clone.clone.1 | custom fusion | bytes 4194320 | tf_op jit(solution)/shard_map/while/body/eval_jaxpr/gather | solution.py:70
  168.7 10.8 %fusion.57 = f32[16,256,1024]{2,1,0:T(8,128)} fusion(bf16[1024,16,64]{2,1,0:T(8,128)(2,1)} %bitcast.78, bf16[4,256,16,64]{1,3,2,0:T(8,128)(2,1)S(1)} %get-tuple-element.171, s32[]{:T(128)} %get-tuple-element.158), kind=kOutput, calls=%fused_computation.13.clone.1 | convolution fusion | flops 536870912 | bytes 19398660 | tf_op jit(solution)/shard_map/while/body/eval_jaxpr/qhd,khd->hqk/dot_general | solution.py:28
  179.5 0.7 dynamic_slice.31
  180.1 0.7 iota_compare_fusion.2
  180.9 18.3 %fusion.58 = (f32[16,256]{1,0:T(8,128)S(1)}, f32[16,256,1024]{2,1,0:T(8,128)}) fusion(f32[16,256,1024]{2,1,0:T(8,128)} %fusion.57, pred[1024]{0:T(1024)(128)(4,1)S(1)} %broadcast_in_dim.55), kind=kOutput, calls=%fused_computation.50.clone.1 | output fusion | flops 25166848 | bytes 33571840 | tf_op jit(solution)/shard_map/while/body/eval_jaxpr/sub | solution.py:33
  199.3 5.8 %gather_fusion.1 = bf16[4,256,16,64]{3,2,1,0:T(8,128)(2,1)} fusion(bf16[6,256,16,64]{3,2,1,0:T(8,128)(2,1)} %get-tuple-element.169, s32[1024]{0:T(1024)S(1)} %pad_clamp_fusion.2), kind=kCustom, calls=%fused_computation.clone.clone.1 | custom fusion | bytes 4194320 | tf_op jit(solution)/shard_map/while/body/eval_jaxpr/gather | solution.py:71
  205.1 11.5 %fusion.59 = bf16[4,256,16,64]{1,3,2,0:T(8,128)(2,1)} fusion(bf16[4,256,16,64]{1,3,2,0:T(8,128)(2,1)} %get-tuple-element.159, s32[]{:T(128)} %get-tuple-element.158, f32[16,256,1024]{2,1,0:T(8,128)} %get-tuple-element.148, f32[16,256]{1,0:T(8,128)S(1)} %get-tuple-element.149, bf16[1024,16,64]{2,1,0:T(8,128)(2,1)} %bitcast.79), kind=kOutput, calls=%fused_computation.17.clone.1 | convolution fusion | flops 545521664 | bytes 21512704 | tf_op jit(solution)/shard_map/while/body/eval_jaxpr/hqk,khd->qhd/dot_general | solution.py:35
  216.5 5.8 %gather_fusion = bf16[4,256,16,64]{3,2,1,0:T(8,128)(2,1)} fusion(bf16[6,256,16,64]{3,2,1,0:T(8,128)(2,1)} %get-tuple-element.172, s32[1024]{0:T(1024)S(1)} %pad_clamp_fusion.2), kind=kCustom, calls=%fused_computation.1.clone.clone.1 | custom fusion | bytes 4194320 | tf_op jit(solution)/shard_map/while/body/eval_jaxpr/gather | solution.py:70
  222.3 10.8 %fusion.57 = f32[16,256,1024]{2,1,0:T(8,128)} fusion(bf16[1024,16,64]{2,1,0:T(8,128)(2,1)} %bitcast.78, bf16[4,256,16,64]{1,3,2,0:T(8,128)(2,1)S(1)} %get-tuple-element.171, s32[]{:T(128)} %get-tuple-element.158), kind=kOutput, calls=%fused_computation.13.clone.1 | convolution fusion | flops 536870912 | bytes 19398660 | tf_op jit(solution)/shard_map/while/body/eval_jaxpr/qhd,khd->hqk/dot_general | solution.py:28
  233.1 0.7 dynamic_slice.31
  233.7 0.7 iota_compare_fusion.2
  234.5 18.3 %fusion.58 = (f32[16,256]{1,0:T(8,128)S(1)}, f32[16,256,1024]{2,1,0:T(8,128)}) fusion(f32[16,256,1024]{2,1,0:T(8,128)} %fusion.57, pred[1024]{0:T(1024)(128)(4,1)S(1)} %broadcast_in_dim.55), kind=kOutput, calls=%fused_computation.50.clone.1 | output fusion | flops 25166848 | bytes 33571840 | tf_op jit(solution)/shard_map/while/body/eval_jaxpr/sub | solution.py:33
  252.8 5.8 %gather_fusion.1 = bf16[4,256,16,64]{3,2,1,0:T(8,128)(2,1)} fusion(bf16[6,256,16,64]{3,2,1,0:T(8,128)(2,1)} %get-tuple-element.169, s32[1024]{0:T(1024)S(1)} %pad_clamp_fusion.2), kind=kCustom, calls=%fused_computation.clone.clone.1 | custom fusion | bytes 4194320 | tf_op jit(solution)/shard_map/while/body/eval_jaxpr/gather | solution.py:71
  258.6 11.5 %fusion.59 = bf16[4,256,16,64]{1,3,2,0:T(8,128)(2,1)} fusion(bf16[4,256,16,64]{1,3,2,0:T(8,128)(2,1)} %get-tuple-element.159, s32[]{:T(128)} %get-tuple-element.158, f32[16,256,1024]{2,1,0:T(8,128)} %get-tuple-element.148, f32[16,256]{1,0:T(8,128)S(1)} %get-tuple-element.149, bf16[1024,16,64]{2,1,0:T(8,128)(2,1)} %bitcast.79), kind=kOutput, calls=%fused_computation.17.clone.1 | convolution fusion | flops 545521664 | bytes 21512704 | tf_op jit(solution)/shard_map/while/body/eval_jaxpr/hqk,khd->qhd/dot_general | solution.py:35
  270.1 3.5 copy.33
  273.6 0.5 copy.38
  274.1 2.5 add_convert_fusion
  276.6 2.2 copy.34
  278.8 82.4 %all_to_all.18 = bf16[4,2,128,1024]{3,1,0,2:T(2,128)(2,1)S(1)} all-to-all(bf16[4,2,128,1024]{3,1,0,2:T(2,128)(2,1)S(1)} %copy.34), channel_id=1, replica_groups=mesh['clip'=2,'tile'=16] {'tile'}, dimensions={2} | all-to-all | bytes 4194304 | tf_op jit(solution)/shard_map/all_to_all | solution.py:80
  361.3 3.6 copy.35
  (30 shorter events, 0.3 us)
Async XLA Ops:
  0.0 15.3 %copy-start = (bf16[1024,1024]{1,0:T(8,128)(2,1)S(1)}, bf16[1024,1024]{1,0:T(8,128)(2,1)}, u32[]{:S(2)}) copy-start(bf16[1024,1024]{1,0:T(8,128)(2,1)} %param.14) | copy-start | bytes 6291460
  10.3 21.5 %collective-permute-start = (bf16[1,2,256,2048]{2,3,1,0:T(8,128)(2,1)}, bf16[1,2,256,2048]{2,3,1,0:T(8,128)(2,1)}, u32[]{:S(2)}, u32[]{:S(2)}) collective-permute-start(bf16[1,2,256,2048]{2,3,1,0:T(8,128)(2,1)} %copy.26), channel_id=1, source_target_pairs={{0,1},{1,2},{2,3},{3,4},{4,5},{5,6},{6,7},{7,8},{8,9},{9,10},{10,1... | collective-permute-start | bytes 6291464 | tf_op jit(solution)/shard_map/ppermute | solution.py:17
  14.0 17.8 %collective-permute-start.1 = (bf16[1,2,256,2048]{2,3,1,0:T(8,128)(2,1)}, bf16[1,2,256,2048]{2,3,1,0:T(8,128)(2,1)}, u32[]{:S(2)}, u32[]{:S(2)}) collective-permute-start(bf16[1,2,256,2048]{2,3,1,0:T(8,128)(2,1)} %copy.26), channel_id=1, source_target_pairs={{1,0},{2,1},{3,2},{4,3},{5,4},{6,5},{7,6},{8,7},{9,8},{10,9},{11,1... | collective-permute-start | bytes 6291464 | tf_op jit(solution)/shard_map/ppermute | solution.py:19
  26.9 4.9 %copy-start.2 = (s32[1,4,4]{2,1,0:T(4,128)S(1)}, s32[1,4,4]{2,1,0:T(4,128)}, u32[]{:S(2)}) copy-start(s32[1,4,4]{2,1,0:T(4,128)} %param.12) | copy-start | bytes 196
  47.2 8.5 %copy-start.5 = (s32[1,4]{1,0:T(1,128)S(1)}, s32[1,4]{1,0:T(1,128)}, u32[]{:S(2)}) copy-start(s32[1,4]{1,0:T(1,128)} %param.13) | copy-start | bytes 52
  270.1 4.0 %copy-start.3 = (bf16[4,2,128,1024]{3,2,1,0:T(8,128)(2,1)S(1)}, bf16[4,2,128,1024]{3,2,1,0:T(8,128)(2,1)}, u32[]{:S(2)}) copy-start(bf16[4,2,128,1024]{3,2,1,0:T(8,128)(2,1)} %param.10) | copy-start | bytes 6291460
  270.1 4.0 %copy-start.4 = (bf16[1024,1024]{1,0:T(8,128)(2,1)S(1)}, bf16[1024,1024]{1,0:T(8,128)(2,1)}, u32[]{:S(2)}) copy-start(bf16[1024,1024]{1,0:T(8,128)(2,1)} %param.17) | copy-start | bytes 6291460
  276.6 88.2 %copy-start.1 = (bf16[1024,1024]{1,0:T(8,128)(2,1)S(1)}, bf16[1024,1024]{1,0:T(8,128)(2,1)}, u32[]{:S(2)}) copy-start(bf16[1024,1024]{1,0:T(8,128)(2,1)} %param.14) | copy-start | bytes 6291460
where the time goes:
time: 366 us; the launch traced here: 365 us
  matrix products  103 us (28%)
  local copies, waits for them, and re-layouts  94.5 us (26%)
  blocking collectives  82.4 us (23%)
  other arithmetic  79.8 us (22%)
  starting transfers between devices  5 us (1%)
    all_to_all x1, blocking collectives, shards(): lax.all_to_all(mixed, 'tile', split_axis=2, concat_axis=1, tiled=True)  82.4 us
    sub x4, other arithmetic, attend(): exp_terms = jnp.exp(scores - row_max)  73.3 us
    dot_general x4, matrix products, attend(): jnp.einsum('hqk,khd->qhd', probabilities, values, preferred_element_type=...  45.8 us
    dot_general x4, matrix products, attend(): jnp.einsum('qhd,khd->hqk', queries, keys, preferred_element_type=jnp.floa...  43 us
    gather x4, local copies, waits for them, and re-layouts, per_frame(): value_table[chosen].reshape(slot_count * block_len, head_count, head_dim)  23.2 us
    gather x4, local copies, waits for them, and re-layouts, per_frame(): key_table[chosen].reshape(slot_count * block_len, head_count, head_dim)  23.2 us
    unnamed x16, local copies, waits for them, and re-layouts  22.4 us
  transfers between devices with their start and end apart: 2, of which 0 were waited for; matrix products, arithmetic and copies ran while one was open for 5% of the time, Pallas kernels for 0%

commit v1 on v0

v1 whole, which is shorter than its diff:
```python
import functools

import jax
import jax.numpy as jnp
from jax import lax
from jax.experimental import pallas as pl
from jax.experimental.pallas import tpu as pltpu
from jax.sharding import PartitionSpec as P

HEADS = 16
PAIR = 128
CHUNK = 256
F32 = jnp.float32
BF16 = jnp.bfloat16


def kernel(
    tiles, exchange, col_count,
    matches, counts, frames_in, keys_in, wq_in, wk_in, wv_in, wo_in,
    out,
    frames, stills, wq, wk, wv, wo, queries, key_table, value_table, context, stage,
    load_sem, halo_send, halo_recv, send_sem, recv_sem, own_sem,
):
    frame_count, block_len, model_dim = frames.shape
    key_count = stills.shape[1] // block_len
    slot_count = matches.shape[2]
    head_dim = model_dim // HEADS
    pair_count = model_dim // PAIR
    chunk_count = model_dim // CHUNK
    rows = block_len // col_count
    cols = col_count // tiles
    me = lax.axis_index("tile")

    loads = [
        pltpu.make_async_copy(src, dst, load_sem.at[i])
        for i, (src, dst) in enumerate(
            [
                (wq_in, wq), (frames_in, frames), (keys_in, stills.at[1]),
                (wk_in, wk), (wv_in, wv), (wo_in, wo),
            ]
        )
    ]
    for load in loads:
        load.start()

    barrier = pltpu.get_barrier_semaphore()

    def greet(step, carry):
        other = lax.rem(me + step, tiles)
        pl.semaphore_signal(
            barrier, inc=1, device_id={"tile": other}, device_id_type=pl.DeviceIdType.MESH
        )
        return carry

    lax.fori_loop(1, tiles, greet, 0)
    pl.semaphore_wait(barrier, tiles - 1)

    def halo(slot, other):
        return pltpu.make_async_remote_copy(
            src_ref=keys_in, dst_ref=stills.at[slot],
            send_sem=halo_send.at[slot], recv_sem=halo_recv.at[slot],
            device_id={"tile": other}, device_id_type=pl.DeviceIdType.MESH,
        )

    @pl.when(me < tiles - 1)
    def _():
        halo(0, me + 1).start()

    @pl.when(me > 0)
    def _():
        halo(2, me - 1).start()

    def fill(block, carry):
        one = jnp.where(block < 3 * key_count, 1.0, 0.0).astype(BF16)
        for pair in range(pair_count):
            value_table[block, :, pl.ds(pair * 2 * PAIR + PAIR, PAIR)] = jnp.full(
                (block_len, PAIR), 1.0, F32
            ).astype(BF16) * one
        return carry

    lax.fori_loop(0, 3 * key_count + 1, fill, 0)
    for pair in range(pair_count):
        value_table[3 * key_count, :, pl.ds(pair * 2 * PAIR, PAIR)] = jnp.zeros(
            (block_len, PAIR), BF16
        )

    loads[0].wait()
    loads[1].wait()
    lane = lax.broadcasted_iota(jnp.int32, (block_len, CHUNK), 1)
    even = lax.rem(lane, PAIR) < head_dim

    def project_queries(step, carry):
        frame, chunk = step // chunk_count, lax.rem(step, chunk_count)
        at = pl.ds(pl.multiple_of(chunk * CHUNK, CHUNK), CHUNK)
        q = jnp.dot(frames[frame], wq[:, at], preferred_element_type=F32)
        q = q * head_dim ** (-0.5)
        queries[frame, 0:block_len, at] = jnp.where(even, q, 0.0).astype(BF16)
        queries[frame, block_len : 2 * block_len, at] = jnp.where(even, 0.0, q).astype(BF16)
        return carry

    lax.fori_loop(0, frame_count * chunk_count, project_queries, 0)

    def project_stills(slot):
        def step(chunk, carry):
            at = pl.ds(pl.multiple_of(chunk * CHUNK, CHUNK), CHUNK)
            k = jnp.dot(stills[slot], wk[:, at], preferred_element_type=F32).astype(BF16)
            v = jnp.dot(stills[slot], wv[:, at], preferred_element_type=F32).astype(BF16)
            for key in range(key_count):
                part = slice(key * block_len, (key + 1) * block_len)
                block = slot * key_count + key
                key_table[block, :, at] = k[part]
                for pair in range(CHUNK // PAIR):
                    to = pl.multiple_of(chunk * 2 * CHUNK + pair * 2 * PAIR, PAIR)
                    value_table[block, :, pl.ds(to, PAIR)] = v[part, pair * PAIR : (pair + 1) * PAIR]
            return carry

        lax.fori_loop(0, chunk_count, step, 0)

    for load in loads[2:5]:
        load.wait()
    project_stills(1)

    @pl.when(me > 0)
    def _():
        halo(0, me - 1).wait_recv()
        project_stills(0)

    @pl.when(me < tiles - 1)
    def _():
        halo(2, me + 1).wait_recv()
        project_stills(2)

    loads[5].wait()
    pair_lane = lax.broadcasted_iota(jnp.int32, (block_len, PAIR), 1) < head_dim

    def send(frame, other, source):
        return pltpu.make_async_remote_copy(
            src_ref=stage.at[frame, other], dst_ref=out.at[frame, source],
            send_sem=send_sem.at[frame, other], recv_sem=recv_sem.at[frame, source],
            device_id={"tile": other}, device_id_type=pl.DeviceIdType.MESH,
        )

    def keep(frame):
        return pltpu.make_async_copy(stage.at[frame, me], out.at[frame, me], own_sem.at[frame])

    def one_frame(frame, carry):
        key_at, value_at = [], []
        for slot in range(slot_count):
            used = slot < counts[0, frame]
            chosen = jnp.where(used, matches[0, frame, slot], matches[0, frame, 0])
            block = lax.rem(chosen, 3) * key_count + lax.div(chosen, 3)
            key_at.append(block)
            value_at.append(jnp.where(used, block, 3 * key_count))

        def one_pair(pair, carry):
            at = pl.ds(pl.multiple_of(pair * PAIR, PAIR), PAIR)
            wide = pl.ds(pl.multiple_of(pair * 2 * PAIR, 2 * PAIR), 2 * PAIR)
            halves = []
            for half in range(2):
                q = queries[frame, half * block_len : (half + 1) * block_len, at]
                scores = [
                    lax.dot_general(
                        q, key_table[k, :, at], (((1,), (1,)), ((), ())), preferred_element_type=F32
                    )
                    for k in key_at
                ]
                row_max = jnp.max(functools.reduce(jnp.maximum, scores), axis=1, keepdims=True)
                total = None
                for score, v in zip(scores, value_at):
                    p = jnp.exp(score - row_max).astype(BF16)
                    term = jnp.dot(p, value_table[v, :, wide], preferred_element_type=F32)
                    total = term if total is None else total + term
                halves.append(total[:, :PAIR] / total[:, PAIR:])
            context[:, at] = jnp.where(pair_lane, halves[0], halves[1]).astype(BF16)
            return carry

        lax.fori_loop(0, pair_count, one_pair, 0)

        for chunk in range(chunk_count):
            at = slice(chunk * CHUNK, (chunk + 1) * CHUNK)
            update = jnp.dot(context[...], wo[:, at], preferred_element_type=F32)
            mixed = frames[frame, :, at].astype(F32) + update
            if exchange:
                for other in range(tiles):
                    piece = [
                        mixed[row * col_count + other * cols : row * col_count + (other + 1) * cols]
                        for row in range(rows)
                    ]
                    stage[frame, other, :, at] = jnp.concatenate(piece, axis=0).astype(BF16)
            else:
                stage[frame, 0, :, at] = mixed.astype(BF16)

        if exchange:

            def start(step, carry):
                send(frame, lax.rem(me + step, tiles), me).start()
                return carry

            lax.fori_loop(1, tiles, start, 0)
            keep(frame).start()
        else:
            pltpu.make_async_copy(stage.at[frame, 0], out.at[frame], own_sem.at[frame]).start()
        return carry

    lax.fori_loop(0, frame_count, one_frame, 0)

    @pl.when(me < tiles - 1)
    def _():
        halo(0, me + 1).wait_send()

    @pl.when(me > 0)
    def _():
        halo(2, me - 1).wait_send()

    def finish(frame, carry):
        if exchange:

            def end(step, carry):
                other = lax.rem(me + step, tiles)
                send(frame, other, me).wait_send()
                send(frame, other, other).wait_recv()
                return carry

            lax.fori_loop(1, tiles, end, 0)
            keep(frame).wait()
        else:
            pltpu.make_async_copy(stage.at[frame, 0], out.at[frame], own_sem.at[frame]).wait()
        return carry

    lax.fori_loop(0, frame_count, finish, 0)


def shards(tiles, frames, keyframes, matches, counts, w_query, w_key, w_value, w_out):
    frame_count, row_count, col_count, model_dim = frames.shape
    key_count = keyframes.shape[0]
    block_len = row_count * col_count
    slots = matches.shape[2]
    cols = col_count // tiles
    exchange = cols % 8 == 0
    pieces = tiles if exchange else 1
    piece_len = block_len // pieces
    if exchange:
        out_shape = (frame_count, tiles, piece_len, model_dim)
    else:
        out_shape = (frame_count, block_len, model_dim)
    weight = pltpu.VMEM((model_dim, model_dim), BF16)
    products = (4 * frame_count + 12 * key_count) * block_len * model_dim * model_dim
    products += 4 * frame_count * slots * block_len * block_len * model_dim
    mixed = pl.pallas_call(
        functools.partial(kernel, tiles, exchange, col_count),
        out_shape=jax.ShapeDtypeStruct(out_shape, BF16),
        in_specs=[pl.BlockSpec(memory_space=pltpu.SMEM)] * 2 + [pl.BlockSpec(memory_space=pl.ANY)] * 6,
        out_specs=pl.BlockSpec(memory_space=pl.ANY),
        scratch_shapes=[
            pltpu.VMEM((frame_count, block_len, model_dim), BF16),
            pltpu.VMEM((3, key_count * block_len, model_dim), BF16),
            weight, weight, weight, weight,
            pltpu.VMEM((frame_count, 2 * block_len, model_dim), BF16),
            pltpu.VMEM((3 * key_count, block_len, model_dim), BF16),
            pltpu.VMEM((3 * key_count + 1, block_len, 2 * model_dim), BF16),
            pltpu.VMEM((block_len, model_dim), BF16),
            pltpu.VMEM((frame_count, pieces, piece_len, model_dim), BF16),
            pltpu.SemaphoreType.DMA((6,)),
            pltpu.SemaphoreType.DMA((3,)),
            pltpu.SemaphoreType.DMA((3,)),
            pltpu.SemaphoreType.DMA((frame_count, pieces)),
            pltpu.SemaphoreType.DMA((frame_count, pieces)),
            pltpu.SemaphoreType.DMA((frame_count,)),
        ],
        compiler_params=pltpu.CompilerParams(
            collective_id=0, has_side_effects=True, vmem_limit_bytes=52 * 1024 * 1024
        ),
        cost_estimate=pl.CostEstimate(
            flops=products, bytes_accessed=16 * 1024 * 1024,
            transcendentals=frame_count * slots * HEADS * block_len * block_len,
        ),
        name="attend_and_relay",
    )(
        matches, counts,
        frames.reshape(frame_count, block_len, model_dim),
        keyframes.reshape(key_count * block_len, model_dim),
        w_query, w_key, w_value, w_out,
    )
    if exchange:
        return mixed.reshape(frame_count, tiles * row_count, cols, model_dim)
    mixed = mixed.reshape(frame_count, row_count, col_count, model_dim)
    return lax.all_to_all(mixed, "tile", split_axis=2, concat_axis=1, tiled=True)


def solution(mesh):
    placed = (
        P("clip", "tile", None, None),
        P("clip", "tile", None, None),
        P("tile", "clip", None),
        P("tile", "clip"),
        P(),
        P(),
        P(),
        P(),
    )
    return jax.shard_map(
        functools.partial(shards, mesh.shape["tile"]),
        mesh=mesh, in_specs=placed, out_specs=P("clip", None, "tile", None), check_vma=False,
    )
```

time: 366 us -> 89.8 us (0.25)
  matrix products: 103 us -> 0 us
  local copies, waits for them, and re-layouts: 94.5 us -> 5.64 us
  Pallas kernels: 0 us -> 83.8 us
  blocking collectives: 82.4 us -> 0 us
  other arithmetic: 79.8 us -> 0 us
  starting transfers between devices: 5 us -> 0 us
    dot_general x11 -> x0, matrix products: 103 us -> none  [the longest x4 45.8 us: attend(): jnp.einsum('hqk,khd->qhd', probabilities, values, preferred_element_type=...]
    pallas_call x0 -> x1, Pallas kernels: none -> 83.8 us  [shards(): pl.pallas_call(functools.partial(kernel, tiles, exchange, col_count), out...]
    all_to_all x1 -> x0, blocking collectives: 82.4 us -> none  [shards(): lax.all_to_all(mixed, 'tile', split_axis=2, concat_axis=1, tiled=True)]
    sub x4 -> x0, other arithmetic: 73.3 us -> none  [attend(): exp_terms = jnp.exp(scores - row_max)]
    gather x8 -> x0, local copies, waits for them, and re-layouts: 46.4 us -> none  [the longest x4 23.2 us: per_frame(): value_table[chosen].reshape(slot_count * block_len, head_count, head_dim)]
    unnamed x16 -> x7, local copies, waits for them, and re-layouts: 22.4 us -> 5.64 us
    reshape x3 -> x0, local copies, waits for them, and re-layouts: 12.5 us -> none  [the longest x1 6.35 us: shards(): query = query.reshape(frame_count, block_len, head_count, head_dim)]
    ppermute x2 -> x0, starting transfers between devices: 5 us -> none  [the longest x1 3.72 us: with_halo(): lax.ppermute(tail, axis, [(i, (i + 1) % count) for i in range(ends)])]
  transfers between devices with their start and end apart: 2 -> 0, of which waited for: 0 -> 0; matrix products, arithmetic and copies ran while one was open for 5% -> 0% of each run, Pallas kernels for 0% -> 0%
where the time goes in v1:
time: 89.8 us; the launch traced here: 89.4 us
  Pallas kernels  83.8 us (93%)
  local copies, waits for them, and re-layouts  5.64 us (6%)
    pallas_call x1, Pallas kernels, shards(): pl.pallas_call(functools.partial(kernel, tiles, exchange, col_count), out...  83.8 us
    unnamed x7, local copies, waits for them, and re-layouts  5.64 us

profile of v1, /device:TPU:0, one launch (start us, length us, event | category | flops | bytes accessed | tf_op | source)
XLA Modules:
  0.0 89.4 jit_solution(11769508988320980759)
XLA Ops:
  0.0 0.0 copy-start
  0.0 1.2 %copy-done = bf16[2,2,128,1024]{3,2,1,0:T(8,128)(2,1)S(1)} copy-done((bf16[2,2,128,1024]{3,2,1,0:T(8,128)(2,1)S(1)}, bf16[2,2,128,1024]{3,2,1,0:T(8,128)(2,1)}, u32[]{:S(2)}) %copy-start) | copy-done | bytes 1048600
  1.2 0.0 copy-start.1
  1.2 0.7 copy-done.1
  1.9 0.0 copy-start.2
  1.9 0.7 copy-done.2
  2.6 83.8 %attend_and_relay.1 = bf16[4,16,16,1024]{3,2,1,0:T(8,128)(2,1)} custom-call(s32[1,4,4]{2,1,0:T(4,128)S(1)} %copy-done.1, s32[1,4]{1,0:T(1,128)S(1)} %copy-done.2, bf16[4,256,1024]{2,1,0:T(8,128)(2,1)} %bitcast.5, bf16[512,1024]{1,0:T(8,128)(2,1)S(1)} %bitcast.3, bf16[1024,1024]{1,0:T(8,128)(2,1)} %wq_in.1, bf16[1024,1024]{1,0:T(8,128)(2,1)} %wk_in.1, ...), custom_call_target="tpu_custom_call" | custom-call | flops 15032385536 | bytes 16777216 | tf_op jit(solution)/shard_map/attend_and_relay/pallas_call | solution.py:249
  86.3 3.1 %copy.10 = bf16[4,32,8,1024]{3,2,1,0:T(8,128)(2,1)} copy(bf16[4,32,8,1024]{3,2,1,0:T(8,128)(2,1)} %bitcast.4) | data formatting | bytes 4194304
Async XLA Ops:
  0.0 1.2 %copy-start = (bf16[2,2,128,1024]{3,2,1,0:T(8,128)(2,1)S(1)}, bf16[2,2,128,1024]{3,2,1,0:T(8,128)(2,1)}, u32[]{:S(2)}) copy-start(bf16[2,2,128,1024]{3,2,1,0:T(8,128)(2,1)} %param.9) | copy-start | bytes 3145732
  1.2 0.7 copy-start.1
  1.9 0.7 copy-start.2

commit v2 on v1

--- a/solution.py
+++ b/solution.py
@@ -9,16 +9,18 @@
 
 HEADS = 16
 PAIR = 128
-CHUNK = 256
+EARLY_QUERIES = 1
+CHUNK = 512
 F32 = jnp.float32
 BF16 = jnp.bfloat16
 
 
 def kernel(
     tiles, exchange, col_count,
-    matches, counts, frames_in, keys_in, wq_in, wk_in, wv_in, wo_in,
+    matches_in, counts_in, frames_in, keys_in, wq_in, wk_in, wv_in, wo_in,
     out,
-    frames, stills, wq, wk, wv, wo, queries, key_table, value_table, context, stage,
+    matches, counts, frames, stills, wq, wk, wv, wo, queries, key_table, value_table, context,
+    stage, scores_even, scores_odd, max_even, max_odd, early_total, early_max,
     load_sem, halo_send, halo_recv, send_sem, recv_sem, own_sem,
 ):
     frame_count, block_len, model_dim = frames.shape
@@ -37,6 +39,7 @@
             [
                 (wq_in, wq), (frames_in, frames), (keys_in, stills.at[1]),
                 (wk_in, wk), (wv_in, wv), (wo_in, wo),
+                (matches_in, matches), (counts_in, counts),
             ]
         )
     ]
@@ -55,20 +58,34 @@
     lax.fori_loop(1, tiles, greet, 0)
     pl.semaphore_wait(barrier, tiles - 1)
 
-    def halo(slot, other):
+    odd = lax.rem(me, 2)
+    partners = ((me + 1 - 2 * odd, 2 - 2 * odd), (me - 1 + 2 * odd, 2 * odd))
+    far = partners[1][0]
+    has_far = (far >= 0) & (far < tiles)
+
+    def halo(kind, key):
+        part = pl.ds(key * block_len, block_len)
         return pltpu.make_async_remote_copy(
-            src_ref=keys_in, dst_ref=stills.at[slot],
-            send_sem=halo_send.at[slot], recv_sem=halo_recv.at[slot],
-            device_id={"tile": other}, device_id_type=pl.DeviceIdType.MESH,
-        )
-
-    @pl.when(me < tiles - 1)
+            src_ref=keys_in.at[part], dst_ref=stills.at[partners[1 - kind][1], part],
+            send_sem=halo_send.at[kind, key], recv_sem=halo_recv.at[kind, key],
+            device_id={"tile": partners[kind][0]}, device_id_type=pl.DeviceIdType.MESH,
+        )
+
+    def arrival(kind, key):
+        part = pl.ds(key * block_len, block_len)
+        return pltpu.make_async_remote_copy(
+            src_ref=keys_in.at[part], dst_ref=stills.at[partners[kind][1], part],
+            send_sem=halo_send.at[kind, key], recv_sem=halo_recv.at[kind, key],
+            device_id={"tile": partners[kind][0]}, device_id_type=pl.DeviceIdType.MESH,
+        )
+
+    @pl.when(has_far)
     def _():
-        halo(0, me + 1).start()
-
-    @pl.when(me > 0)
-    def _():
-        halo(2, me - 1).start()
+        for key in range(key_count):
+            halo(1, key).start()
+
+    for key in range(key_count):
+        halo(0, key).start()
 
     def fill(block, carry):
         one = jnp.where(block < 3 * key_count, 1.0, 0.0).astype(BF16)
@@ -89,25 +106,29 @@
     lane = lax.broadcasted_iota(jnp.int32, (block_len, CHUNK), 1)
     even = lax.rem(lane, PAIR) < head_dim
 
-    def project_queries(step, carry):
-        frame, chunk = step // chunk_count, lax.rem(step, chunk_count)
-        at = pl.ds(pl.multiple_of(chunk * CHUNK, CHUNK), CHUNK)
-        q = jnp.dot(frames[frame], wq[:, at], preferred_element_type=F32)
-        q = q * head_dim ** (-0.5)
-        queries[frame, 0:block_len, at] = jnp.where(even, q, 0.0).astype(BF16)
-        queries[frame, block_len : 2 * block_len, at] = jnp.where(even, 0.0, q).astype(BF16)
-        return carry
-
-    lax.fori_loop(0, frame_count * chunk_count, project_queries, 0)
-
-    def project_stills(slot):
+    def project_queries(frame):
         def step(chunk, carry):
             at = pl.ds(pl.multiple_of(chunk * CHUNK, CHUNK), CHUNK)
-            k = jnp.dot(stills[slot], wk[:, at], preferred_element_type=F32).astype(BF16)
-            v = jnp.dot(stills[slot], wv[:, at], preferred_element_type=F32).astype(BF16)
-            for key in range(key_count):
+            q = jnp.dot(frames[frame], wq[:, at], preferred_element_type=F32)
+            q = q * head_dim ** (-0.5)
+            queries[frame, 0:block_len, at] = jnp.where(even, q, 0.0).astype(BF16)
+            queries[frame, block_len : 2 * block_len, at] = jnp.where(even, 0.0, q).astype(BF16)
+            return carry
+
+        lax.fori_loop(0, chunk_count, step, 0)
+
+    for frame in range(EARLY_QUERIES):
+        project_queries(frame)
+
+    def project_stills(slot, first, count):
+        def step(chunk, carry):
+            at = pl.ds(pl.multiple_of(chunk * CHUNK, CHUNK), CHUNK)
+            tokens = stills[slot, first * block_len : (first + count) * block_len, :]
+            k = jnp.dot(tokens, wk[:, at], preferred_element_type=F32).astype(BF16)
+            v = jnp.dot(tokens, wv[:, at], preferred_element_type=F32).astype(BF16)
+            for key in range(count):
                 part = slice(key * block_len, (key + 1) * block_len)
-                block = slot * key_count + key
+                block = slot * key_count + first + key
                 key_table[block, :, at] = k[part]
                 for pair in range(CHUNK // PAIR):
                     to = pl.multiple_of(chunk * 2 * CHUNK + pair * 2 * PAIR, PAIR)
@@ -118,19 +139,13 @@
 
     for load in loads[2:5]:
         load.wait()
-    project_stills(1)
-
-    @pl.when(me > 0)
-    def _():
-        halo(0, me - 1).wait_recv()
-        project_stills(0)
-
-    @pl.when(me < tiles - 1)
-    def _():
-        halo(2, me + 1).wait_recv()
-        project_stills(2)
-
-    loads[5].wait()
+    project_stills(1, 0, key_count)
+    for key in range(key_count):
+        arrival(0, key).wait_recv()
+    project_stills(partners[0][1], 0, key_count)
+
+    for load in loads[5:]:
+        load.wait()
     pair_lane = lax.broadcasted_iota(jnp.int32, (block_len, PAIR), 1) < head_dim
 
     def send(frame, other, source):
@@ -140,42 +155,89 @@
             device_id={"tile": other}, device_id_type=pl.DeviceIdType.MESH,
         )
 
+    def partner(step):
+        if tiles & (tiles - 1):
+            return lax.rem(me + step, tiles)
+        other, bit = 0, 1
+        while bit < tiles:
+            other = other + lax.rem(me // bit + step // bit, 2) * bit
+            bit *= 2
+        return other
+
     def keep(frame):
         return pltpu.make_async_copy(stage.at[frame, me], out.at[frame, me], own_sem.at[frame])
 
-    def one_frame(frame, carry):
-        key_at, value_at = [], []
-        for slot in range(slot_count):
-            used = slot < counts[0, frame]
-            chosen = jnp.where(used, matches[0, frame, slot], matches[0, frame, 0])
-            block = lax.rem(chosen, 3) * key_count + lax.div(chosen, 3)
-            key_at.append(block)
-            value_at.append(jnp.where(used, block, 3 * key_count))
+    def attend(frame, keys, values, early=False, late=False):
+        def score(pair, half, scores, top):
+            at = pl.ds(pl.multiple_of(pair * PAIR, PAIR), PAIR)
+            q = queries[frame, half * block_len : (half + 1) * block_len, at]
+            most = None
+            for slot, key in enumerate(keys):
+                s = lax.dot_general(
+                    q, key_table[key, :, at], (((1,), (1,)), ((), ())), preferred_element_type=F32
+                )
+                scores[:, slot * block_len : (slot + 1) * block_len] = s
+                for piece in range(block_len // PAIR):
+                    part = s[:, piece * PAIR : (piece + 1) * PAIR]
+                    most = part if most is None else jnp.maximum(most, part)
+            most = jnp.broadcast_to(jnp.max(most, axis=1, keepdims=True), top.shape)
+            if late:
+                most = jnp.maximum(most, early_max[pair * 2 + half])
+            top[...] = most
+
+        def gather(pair, half, scores, top):
+            wide = pl.ds(pl.multiple_of(pair * 2 * PAIR, 2 * PAIR), 2 * PAIR)
+            most = top[...]
+            total = None
+            if late:
+                scale = jnp.exp(early_max[pair * 2 + half] - most)
+                total = early_total[pair * 2 + half] * jnp.concatenate([scale, scale], axis=1)
+            p = jnp.concatenate(
+                [
+                    jnp.exp(scores[:, at : at + PAIR] - most).astype(BF16)
+                    for at in range(0, len(values) * block_len, PAIR)
+                ],
+                axis=1,
+            )
+            v = jnp.concatenate([value_table[value, :, wide] for value in values], axis=0)
+            term = jnp.dot(p, v, preferred_element_type=F32)
+            total = term if total is None else total + term
+            if early:
+                early_total[pair * 2 + half] = total
+                early_max[pair * 2 + half] = most
+                return None
+            return total[:, :PAIR] / total[:, PAIR:]
+
+        score(0, 0, scores_even, max_even)
 
         def one_pair(pair, carry):
             at = pl.ds(pl.multiple_of(pair * PAIR, PAIR), PAIR)
-            wide = pl.ds(pl.multiple_of(pair * 2 * PAIR, 2 * PAIR), 2 * PAIR)
-            halves = []
-            for half in range(2):
-                q = queries[frame, half * block_len : (half + 1) * block_len, at]
-                scores = [
-                    lax.dot_general(
-                        q, key_table[k, :, at], (((1,), (1,)), ((), ())), preferred_element_type=F32
-                    )
-                    for k in key_at
-                ]
-                row_max = jnp.max(functools.reduce(jnp.maximum, scores), axis=1, keepdims=True)
-                total = None
-                for score, v in zip(scores, value_at):
-                    p = jnp.exp(score - row_max).astype(BF16)
-                    term = jnp.dot(p, value_table[v, :, wide], preferred_element_type=F32)
-                    total = term if total is None else total + term
-                halves.append(total[:, :PAIR] / total[:, PAIR:])
-            context[:, at] = jnp.where(pair_lane, halves[0], halves[1]).astype(BF16)
+            score(pair, 1, scores_odd, max_odd)
+            first = gather(pair, 0, scores_even, max_even)
+            score(jnp.minimum(pair + 1, pair_count - 1), 0, scores_even, max_even)
+            second = gather(pair, 1, scores_odd, max_odd)
+            if not early:
+                context[:, at] = jnp.where(pair_lane, first, second).astype(BF16)
             return carry
 
         lax.fori_loop(0, pair_count, one_pair, 0)
 
+    def used(frame, slot):
+        return slot < counts[0, frame]
+
+    def named(frame, position):
+        keys, values = [], []
+        for key in range(key_count):
+            there = jnp.int32(0)
+            for slot in range(slot_count):
+                same = (matches[0, frame, slot] == key * 3 + position) & used(frame, slot)
+                there = there + jnp.where(same, 1, 0)
+            block = position * key_count + key
+            keys.append(jnp.where(there > 0, block, key_count))
+            values.append(jnp.where(there > 0, block, 3 * key_count))
+        return keys, values
+
+    def finish_frame(frame):
         for chunk in range(chunk_count):
             at = slice(chunk * CHUNK, (chunk + 1) * CHUNK)
             update = jnp.dot(context[...], wo[:, at], preferred_element_type=F32)
@@ -193,24 +255,52 @@
         if exchange:
 
             def start(step, carry):
-                send(frame, lax.rem(me + step, tiles), me).start()
+                send(frame, partner(tiles - step), me).start()
                 return carry
 
             lax.fori_loop(1, tiles, start, 0)
             keep(frame).start()
         else:
             pltpu.make_async_copy(stage.at[frame, 0], out.at[frame], own_sem.at[frame]).start()
+
+    def one_frame(frame, carry):
+        keys, values = [], []
+        for slot in range(slot_count):
+            chosen = jnp.where(used(frame, slot), matches[0, frame, slot], matches[0, frame, 0])
+            block = lax.rem(chosen, 3) * key_count + lax.div(chosen, 3)
+            keys.append(block)
+            values.append(jnp.where(used(frame, slot), block, 3 * key_count))
+        if EARLY_QUERIES < frame_count:
+
+            @pl.when(frame >= EARLY_QUERIES)
+            def _():
+                project_queries(frame)
+
+        attend(frame, keys, values)
+        finish_frame(frame)
         return carry
 
-    lax.fori_loop(0, frame_count, one_frame, 0)
-
-    @pl.when(me < tiles - 1)
+    own_keys, own_values = named(0, 1)
+    near_keys, near_values = named(0, partners[0][1])
+    attend(0, own_keys + near_keys, own_values + near_values, early=True)
+
+    @pl.when(has_far)
     def _():
-        halo(0, me + 1).wait_send()
-
-    @pl.when(me > 0)
+        for key in range(key_count):
+            arrival(1, key).wait_recv()
+            project_stills(partners[1][1], key, 1)
+
+    attend(0, *named(0, partners[1][1]), late=True)
+    finish_frame(0)
+    lax.fori_loop(1, frame_count, one_frame, 0)
+
+    @pl.when(has_far)
     def _():
-        halo(2, me - 1).wait_send()
+        for key in range(key_count):
+            halo(1, key).wait_send()
+
+    for key in range(key_count):
+        halo(0, key).wait_send()
 
     def finish(frame, carry):
         if exchange:
@@ -249,9 +339,11 @@
     mixed = pl.pallas_call(
         functools.partial(kernel, tiles, exchange, col_count),
         out_shape=jax.ShapeDtypeStruct(out_shape, BF16),
-        in_specs=[pl.BlockSpec(memory_space=pltpu.SMEM)] * 2 + [pl.BlockSpec(memory_space=pl.ANY)] * 6,
+        in_specs=[pl.BlockSpec(memory_space=pl.ANY)] * 8,
         out_specs=pl.BlockSpec(memory_space=pl.ANY),
         scratch_shapes=[
+            pltpu.SMEM(matches.shape, jnp.int32),
+            pltpu.SMEM(counts.shape, jnp.int32),
             pltpu.VMEM((frame_count, block_len, model_dim), BF16),
             pltpu.VMEM((3, key_count * block_len, model_dim), BF16),
             weight, weight, weight, weight,
@@ -260,15 +352,21 @@
             pltpu.VMEM((3 * key_count + 1, block_len, 2 * model_dim), BF16),
             pltpu.VMEM((block_len, model_dim), BF16),
             pltpu.VMEM((frame_count, pieces, piece_len, model_dim), BF16),
-            pltpu.SemaphoreType.DMA((6,)),
-            pltpu.SemaphoreType.DMA((3,)),
-            pltpu.SemaphoreType.DMA((3,)),
+            pltpu.VMEM((block_len, slots * block_len), F32),
+            pltpu.VMEM((block_len, slots * block_len), F32),
+            pltpu.VMEM((block_len, PAIR), F32),
+            pltpu.VMEM((block_len, PAIR), F32),
+            pltpu.VMEM((HEADS, block_len, 2 * PAIR), F32),
+            pltpu.VMEM((HEADS, block_len, PAIR), F32),
+            pltpu.SemaphoreType.DMA((8,)),
+            pltpu.SemaphoreType.DMA((2, key_count)),
+            pltpu.SemaphoreType.DMA((2, key_count)),
             pltpu.SemaphoreType.DMA((frame_count, pieces)),
             pltpu.SemaphoreType.DMA((frame_count, pieces)),
             pltpu.SemaphoreType.DMA((frame_count,)),
         ],
         compiler_params=pltpu.CompilerParams(
-            collective_id=0, has_side_effects=True, vmem_limit_bytes=52 * 1024 * 1024
+            collective_id=0, has_side_effects=True, vmem_limit_bytes=60 * 1024 * 1024
         ),
         cost_estimate=pl.CostEstimate(
             flops=products, bytes_accessed=16 * 1024 * 1024,

time: 89.8 us -> 83.2 us (0.927)
  Pallas kernels: 83.8 us -> 80 us
  local copies, waits for them, and re-layouts: 5.64 us -> 3.08 us
    pallas_call x1, Pallas kernels: 83.8 us -> 80 us  [shards(): pl.pallas_call(functools.partial(kernel, tiles, exchange, col_count), out...]
    unnamed x7 -> x1, local copies, waits for them, and re-layouts: 5.64 us -> 3.08 us
where the time goes in v2:
time: 83.2 us; the launch traced here: 83 us
  Pallas kernels  80 us (96%)
  local copies, waits for them, and re-layouts  3.08 us (4%)
    pallas_call x1, Pallas kernels, shards(): pl.pallas_call(functools.partial(kernel, tiles, exchange, col_count), out...  80 us
    unnamed x1, local copies, waits for them, and re-layouts  3.08 us

profile of v2, /device:TPU:0, one launch (start us, length us, event | category | flops | bytes accessed | tf_op | source)
XLA Modules:
  0.0 83.0 jit_solution(3953922542923912065)
XLA Ops:
  0.0 80.0 %attend_and_relay.1 = bf16[4,16,16,1024]{3,2,1,0:T(8,128)(2,1)} custom-call(s32[1,4,4]{2,1,0:T(4,128)} %matches_in.1, s32[1,4]{1,0:T(1,128)} %counts_in.1, bf16[4,256,1024]{2,1,0:T(8,128)(2,1)} %bitcast.4, bf16[512,1024]{1,0:T(8,128)(2,1)} %bitcast.5, bf16[1024,1024]{1,0:T(8,128)(2,1)} %wq_in.1, bf16[1024,1024]{1,0:T(8,128)(2,1)} %wk_in.1, ...), custom_call_target="tpu_custom_call" | custom-call | flops 15032385536 | bytes 16777216 | tf_op jit(solution)/shard_map/attend_and_relay/pallas_call | solution.py:339
  80.0 3.1 %copy.10 = bf16[4,32,8,1024]{3,2,1,0:T(8,128)(2,1)} copy(bf16[4,32,8,1024]{3,2,1,0:T(8,128)(2,1)} %bitcast.3) | data formatting | bytes 4194304

commit v3 on v2

--- a/solution.py
+++ b/solution.py
@@ -129,7 +129,7 @@
             for key in range(count):
                 part = slice(key * block_len, (key + 1) * block_len)
                 block = slot * key_count + first + key
-                key_table[block, :, at] = k[part]
+                key_table[block, at, :] = k[part].T
                 for pair in range(CHUNK // PAIR):
                     to = pl.multiple_of(chunk * 2 * CHUNK + pair * 2 * PAIR, PAIR)
                     value_table[block, :, pl.ds(to, PAIR)] = v[part, pair * PAIR : (pair + 1) * PAIR]
@@ -168,59 +168,68 @@
         return pltpu.make_async_copy(stage.at[frame, me], out.at[frame, me], own_sem.at[frame])
 
     def attend(frame, keys, values, early=False, late=False):
-        def score(pair, half, scores, top):
-            at = pl.ds(pl.multiple_of(pair * PAIR, PAIR), PAIR)
-            q = queries[frame, half * block_len : (half + 1) * block_len, at]
-            most = None
-            for slot, key in enumerate(keys):
-                s = lax.dot_general(
-                    q, key_table[key, :, at], (((1,), (1,)), ((), ())), preferred_element_type=F32
-                )
-                scores[:, slot * block_len : (slot + 1) * block_len] = s
-                for piece in range(block_len // PAIR):
-                    part = s[:, piece * PAIR : (piece + 1) * PAIR]
-                    most = part if most is None else jnp.maximum(most, part)
-            most = jnp.broadcast_to(jnp.max(most, axis=1, keepdims=True), top.shape)
-            if late:
-                most = jnp.maximum(most, early_max[pair * 2 + half])
-            top[...] = most
-
-        def gather(pair, half, scores, top):
-            wide = pl.ds(pl.multiple_of(pair * 2 * PAIR, 2 * PAIR), 2 * PAIR)
-            most = top[...]
-            total = None
-            if late:
-                scale = jnp.exp(early_max[pair * 2 + half] - most)
-                total = early_total[pair * 2 + half] * jnp.concatenate([scale, scale], axis=1)
+        def score_block(q, slot, at, scores, most):
+            s = jnp.dot(q, key_table[keys[slot], at, :], preferred_element_type=F32)
+            scores[:, slot * block_len : (slot + 1) * block_len] = s
+            for piece in range(block_len // PAIR):
+                part = s[:, piece * PAIR : (piece + 1) * PAIR]
+                most = part if most is None else jnp.maximum(most, part)
+            return most
+
+        def value_block(slot, wide, scores, most, total):
             p = jnp.concatenate(
                 [
                     jnp.exp(scores[:, at : at + PAIR] - most).astype(BF16)
-                    for at in range(0, len(values) * block_len, PAIR)
+                    for at in range(slot * block_len, (slot + 1) * block_len, PAIR)
                 ],
                 axis=1,
             )
-            v = jnp.concatenate([value_table[value, :, wide] for value in values], axis=0)
-            term = jnp.dot(p, v, preferred_element_type=F32)
-            total = term if total is None else total + term
+            term = jnp.dot(p, value_table[values[slot], :, wide], preferred_element_type=F32)
+            return term if total is None else total + term
+
+        def close(most, pair, top):
+            most = jnp.broadcast_to(jnp.max(most, axis=1, keepdims=True), top.shape)
+            if late:
+                most = jnp.maximum(most, early_max[pair])
+            top[...] = most
+
+        def columns(pair, width):
+            return pl.ds(pl.multiple_of(pair * width, width), width)
+
+        def load_query(pair):
+            return queries[frame, :, columns(pair, PAIR)]
+
+        def step(pair, scores, top, next_pair, next_scores, next_top):
+            most, total, next_most = top[...], None, None
+            q = load_query(next_pair)
+            if late:
+                scale = jnp.exp(early_max[pair] - most)
+                total = early_total[pair] * jnp.concatenate([scale, scale], axis=1)
+            for slot in range(len(keys)):
+                next_most = score_block(q, slot, columns(next_pair, PAIR), next_scores, next_most)
+                total = value_block(slot, columns(pair, 2 * PAIR), scores, most, total)
+            close(next_most, next_pair, next_top)
             if early:
-                early_total[pair * 2 + half] = total
-                early_max[pair * 2 + half] = most
+                early_total[pair] = total
+                early_max[pair] = most
                 return None
-            return total[:, :PAIR] / total[:, PAIR:]
-
-        score(0, 0, scores_even, max_even)
-
-        def one_pair(pair, carry):
-            at = pl.ds(pl.multiple_of(pair * PAIR, PAIR), PAIR)
-            score(pair, 1, scores_odd, max_odd)
-            first = gather(pair, 0, scores_even, max_even)
-            score(jnp.minimum(pair + 1, pair_count - 1), 0, scores_even, max_even)
-            second = gather(pair, 1, scores_odd, max_odd)
-            if not early:
-                context[:, at] = jnp.where(pair_lane, first, second).astype(BF16)
+            each = total[:, :PAIR] / total[:, PAIR:]
+            both = jnp.where(pair_lane, each[:block_len], each[block_len:])
+            context[:, columns(pair, PAIR)] = both.astype(BF16)
+
+        most, q = None, load_query(0)
+        for slot in range(len(keys)):
+            most = score_block(q, slot, columns(0, PAIR), scores_even, most)
+        close(most, 0, max_even)
+
+        def two_pairs(index, carry):
+            pair = index * 2
+            after = jnp.minimum(pair + 2, pair_count - 1)
+            step(pair, scores_even, max_even, pair + 1, scores_odd, max_odd)
+            step(pair + 1, scores_odd, max_odd, after, scores_even, max_even)
             return carry
 
-        lax.fori_loop(0, pair_count, one_pair, 0)
+        lax.fori_loop(0, pair_count // 2, two_pairs, 0)
 
     def used(frame, slot):
         return slot < counts[0, frame]
@@ -348,16 +357,16 @@
             pltpu.VMEM((3, key_count * block_len, model_dim), BF16),
             weight, weight, weight, weight,
             pltpu.VMEM((frame_count, 2 * block_len, model_dim), BF16),
-            pltpu.VMEM((3 * key_count, block_len, model_dim), BF16),
+            pltpu.VMEM((3 * key_count, model_dim, block_len), BF16),
             pltpu.VMEM((3 * key_count + 1, block_len, 2 * model_dim), BF16),
             pltpu.VMEM((block_len, model_dim), BF16),
             pltpu.VMEM((frame_count, pieces, piece_len, model_dim), BF16),
-            pltpu.VMEM((block_len, slots * block_len), F32),
-            pltpu.VMEM((block_len, slots * block_len), F32),
-            pltpu.VMEM((block_len, PAIR), F32),
-            pltpu.VMEM((block_len, PAIR), F32),
-            pltpu.VMEM((HEADS, block_len, 2 * PAIR), F32),
-            pltpu.VMEM((HEADS, block_len, PAIR), F32),
+            pltpu.VMEM((2 * block_len, slots * block_len), F32),
+            pltpu.VMEM((2 * block_len, slots * block_len), F32),
+            pltpu.VMEM((2 * block_len, PAIR), F32),
+            pltpu.VMEM((2 * block_len, PAIR), F32),
+            pltpu.VMEM((HEADS // 2, 2 * block_len, 2 * PAIR), F32),
+            pltpu.VMEM((HEADS // 2, 2 * block_len, PAIR), F32),
             pltpu.SemaphoreType.DMA((8,)),
             pltpu.SemaphoreType.DMA((2, key_count)),
             pltpu.SemaphoreType.DMA((2, key_count)),

time: 83.2 us -> 80.8 us (0.971)
  Pallas kernels: 80 us -> 77.6 us
    pallas_call x1, Pallas kernels: 80 us -> 77.6 us  [shards(): pl.pallas_call(functools.partial(kernel, tiles, exchange, col_count), out...]
where the time goes in v3:
time: 80.8 us; the launch traced here: 80.7 us
  Pallas kernels  77.6 us (96%)
  local copies, waits for them, and re-layouts  3.08 us (4%)
    pallas_call x1, Pallas kernels, shards(): pl.pallas_call(functools.partial(kernel, tiles, exchange, col_count), out...  77.6 us
    unnamed x1, local copies, waits for them, and re-layouts  3.08 us

profile of v3, /device:TPU:0, one launch (start us, length us, event | category | flops | bytes accessed | tf_op | source)
XLA Modules:
  0.0 80.7 jit_solution(17549253500295344143)
XLA Ops:
  0.0 77.6 %attend_and_relay.1 = bf16[4,16,16,1024]{3,2,1,0:T(8,128)(2,1)} custom-call(s32[1,4,4]{2,1,0:T(4,128)} %matches_in.1, s32[1,4]{1,0:T(1,128)} %counts_in.1, bf16[4,256,1024]{2,1,0:T(8,128)(2,1)} %bitcast.4, bf16[512,1024]{1,0:T(8,128)(2,1)} %bitcast.5, bf16[1024,1024]{1,0:T(8,128)(2,1)} %wq_in.1, bf16[1024,1024]{1,0:T(8,128)(2,1)} %wk_in.1, ...), custom_call_target="tpu_custom_call" | custom-call | flops 15032385536 | bytes 16777216 | tf_op jit(solution)/shard_map/attend_and_relay/pallas_call | solution.py:348
  77.6 3.1 %copy.10 = bf16[4,32,8,1024]{3,2,1,0:T(8,128)(2,1)} copy(bf16[4,32,8,1024]{3,2,1,0:T(8,128)(2,1)} %bitcast.3) | data formatting | bytes 4194304
